TPU v7x, 32 devices: a whole 2x2x4 slice. The times are simulated.
32 devices in a mesh: dom: 8 (over z, y), rep: 4 (over x, core).
Axes of the slice: x: 2, y: 2, z: 4, core: 2. Of those that a mesh axis runs over, the one named last changes fastest.
Arguments:
- coords: float32 [8, 3, 8192], P('dom'), may hold values from -6 to 6
- disp: float32 [8, 3, 8192], P('dom'), may hold values from -4 to 4
- mass: float32 [8, 8192], P('dom'), may hold values from 0.5 to 4
- stiffness: float32 [24, 24], replicated, may hold values from -1.25 to 1.25
- elem_nodes: int32 [8, 8, 4096], P('dom', None, 'rep'), may hold values from 0 to 8191
- modulus: float32 [8, 4096], P('dom', 'rep'), may hold values from 0.3 to 3
- surf_nodes: int32 [8, 128, 128], P('dom'), may hold values from 0 to 8191
- block_region: int32 [8, 128], P('dom'), may hold values from 0 to 7, as said below
- face_pos: float32 [8, 64, 3, 128], P('dom'), may hold values from -6 to 6
- face_normal: float32 [8, 64, 3, 128], P('dom'), may hold values from -6 to 6
- tile_slot: int32 [8, 32], P('dom', 'rep'), may hold values from 0 to 255, as said below
- tile_face: int32 [8, 32], P('dom', 'rep'), may hold values from 0 to 63
- tile_weight: bfloat16 [8, 32, 128, 128], P('dom', 'rep'), may hold values from -0.5 to 0.5
- shared_lo: int32 [8, 512], P('dom'), may hold values from 0 to 8191
- shared_hi: int32 [8, 512], P('dom'), may hold values from 0 to 8191
Outputs:
- accel: float32 [8, 3, 8192], P('dom')
Inputs may be any that keep to these rules, and one draw needn't show every extreme that they name: `block_region`: each partition's blocks come in runs of 32: blocks b with equal b // 32 share a box, and the 4 runs go to distinct boxes, so a partition sends at most 32 blocks to one box. Partition s always sends a run to each of the boxes s + 1, s - 1 and s + 8 // 2 (counted round). `tile_slot`: slot source * 32 + c with c < 32, where the source partition sends blocks to this box.
All inputs are finite; a program needn't handle non-finite values.
Results may differ from a plain program's by a relative error of at most 0.0065.
Values may be sent and summed in bfloat16 or wider, within the bound.
No kernel may reach another device: no remote copies, remote signals or barrier semaphores. Data moves between devices by JAX's collectives and lax.ppermute only.
A program may use at most 64 MiB of HBM per device.

v0:
```python
import functools

import jax
import jax.numpy as jnp
from jax import lax
from jax.experimental import pallas as pl
from jax.experimental.pallas import tpu as pltpu
from jax.sharding import PartitionSpec as P

penalty = 4.0
lanes = 128
wide = 256
vmem = pl.BlockSpec(memory_space=pltpu.VMEM)
smem = pl.BlockSpec(memory_space=pltpu.SMEM)
f32 = jnp.float32
bf16 = jnp.bfloat16


def call(body, out_shape, in_specs, out_specs, scratch, flops):
    return pl.pallas_call(
        body,
        out_shape=out_shape,
        in_specs=in_specs,
        out_specs=out_specs,
        scratch_shapes=scratch,
        compiler_params=pltpu.CompilerParams(vmem_limit_bytes=32 * 1024 * 1024),
        cost_estimate=pl.CostEstimate(flops=flops, bytes_accessed=1 << 20, transcendentals=0),
    )


def one_hot(nodes):
    line = lax.broadcasted_iota(jnp.int32, (wide, lanes), 0)
    return jnp.concatenate(
        [jnp.where(line == (row & (wide - 1)), 1.0, 0.0).astype(bf16) for row in nodes], axis=1
    )


def halves(ref, c, tops):
    at = c * 2 * tops
    return jnp.concatenate(
        [ref[pl.ds(at, tops, stride=2)], ref[pl.ds(at + 1, tops, stride=2)]], axis=1
    )


def two_parts(x):
    coarse = x.astype(bf16)
    return [coarse, (x - coarse.astype(f32)).astype(bf16)]


def lookup(tables, nodes):
    tops = tables[0][0].shape[0]
    stacked = jnp.concatenate([part for table in tables for part in table], axis=0)
    found = jnp.dot(stacked, one_hot(nodes), preferred_element_type=f32)
    line = lax.broadcasted_iota(jnp.int32, (tops, lanes), 0)
    values = [[] for _ in tables]
    for i, row in enumerate(nodes):
        match = line == (row >> 8)
        at = 0
        for c, table in enumerate(tables):
            here = found[at : at + tops, i * lanes : (i + 1) * lanes]
            for p in range(1, len(table)):
                here += found[at + p * tops : at + (p + 1) * tops, i * lanes : (i + 1) * lanes]
            at += len(table) * tops
            values[c].append(jnp.sum(jnp.where(match, here, 0.0), axis=0, keepdims=True))
    return values


def node_sums(nodes, values, tops):
    line = lax.broadcasted_iota(jnp.int32, (tops, lanes), 0)
    comps = len(values)
    left = []
    for i, row in enumerate(nodes):
        match = line == (row >> 8)
        coarse = [v[i].astype(bf16).astype(f32) for v in values]
        fine = [v[i] - w for v, w in zip(values, coarse)]
        left.append(
            jnp.concatenate(
                [jnp.where(match, v, 0.0).astype(bf16) for v in coarse + fine], axis=0
            )
        )
    both = lax.dot_general(
        jnp.concatenate(left, axis=1),
        one_hot(nodes),
        (((1,), (1,)), ((), ())),
        preferred_element_type=f32,
    )
    return both[: comps * tops] + both[comps * tops :]


def add_halves(ref, sums, c, tops, row=None):
    at = (c if row is None else row) * 2 * tops
    for half in range(2):
        ref[pl.ds(at + half, tops, stride=2)] += sums[
            c * tops : (c + 1) * tops, half * lanes : (half + 1) * lanes
        ]


def pack_kernel(cap, region_ref, slot_ref, coords_ref, disp_ref, surf_ref, out_ref, stage):
    parts, rows, _ = out_ref.shape
    nblk = surf_ref.shape[1]
    tiles = slot_ref.shape[1]
    tops = coords_ref.shape[0] // 6
    rest = (rows - 3 * cap, lanes)
    lane = lax.broadcasted_iota(jnp.int32, rest, 1)
    line = lax.broadcasted_iota(jnp.int32, rest, 0)
    tail = jnp.zeros(rest, f32)
    for t in range(tiles):
        tail = jnp.where((lane == t) & (line == 0), slot_ref[0, t].astype(f32), tail)
    for q in range(nblk // cap):
        stage[q, 3 * cap :] = tail
    empty = jnp.concatenate([jnp.zeros((3 * cap, lanes), f32), tail], axis=0).astype(bf16)
    for j in range(parts):
        out_ref[j] = empty
    tables = [
        [(halves(coords_ref, c, tops) + halves(disp_ref, c, tops)).astype(bf16)] for c in range(3)
    ]
    size = min(cap, 8)
    for first in range(0, nblk, 8):
        values = lookup(tables, [surf_ref[0, first + i : first + i + 1] for i in range(8)])
        for b in range(first, first + 8, size):
            for c in range(3):
                at = c * cap + b % cap
                stage[b // cap, at : at + size] = jnp.concatenate(
                    values[c][b - first : b - first + size], axis=0
                )
    for q in range(nblk // cap):
        out_ref[region_ref[0, q * cap]] = stage[q].astype(bf16)


def element_kernel(disp_ref, stiff_ref, modulus_ref, nodes_ref, out_ref, local, sums):
    corners, count = nodes_ref.shape[1:]
    tops = disp_ref.shape[0] // 6
    tables = [two_parts(halves(disp_ref, c, tops)) for c in range(3)]
    cuts = [slice(g * lanes, (g + 1) * lanes) for g in range(count // lanes)]
    nodes = [[nodes_ref[0, a : a + 1, cut] for a in range(corners)] for cut in cuts]
    for cut, here in zip(cuts, nodes):
        values = lookup(tables, here)
        for c in range(3):
            local[c * corners : (c + 1) * corners, cut] = jnp.concatenate(values[c], axis=0)
    force = jnp.dot(
        stiff_ref[...], local[...], precision=lax.Precision.HIGHEST, preferred_element_type=f32
    )
    local[...] = -(force * modulus_ref[...])
    for g, (cut, here) in enumerate(zip(cuts, nodes)):
        values = [
            [local[c * corners + a : c * corners + a + 1, cut] for a in range(corners)]
            for c in range(3)
        ]
        added = node_sums(here, values, tops)
        sums[...] = added if g == 0 else sums[...] + added
    out_ref[...] = jnp.zeros_like(out_ref)
    for c in range(3):
        add_halves(out_ref, sums[...], c, tops)


def tile_kernel(
    cap, slot_ref, face_ref, got_ref, pos_ref, normal_ref, weight_ref, after_ref, out_ref, slots_ref, flat
):
    parts, rows, _ = got_ref.shape
    tiles = slot_ref.shape[1]
    for j in range(parts):
        flat[j * rows : (j + 1) * rows] = got_ref[j].astype(f32)
    slots_ref[...] = jnp.concatenate(
        [flat[j * rows + 3 * cap : j * rows + 3 * cap + 1] for j in range(parts)], axis=0
    ).astype(jnp.int32)
    starts = [(slot_ref[0, t] // cap) * rows + slot_ref[0, t] % cap for t in range(tiles)]
    x = jnp.concatenate(
        [flat[pl.ds(at + c * cap, 1)] for c in range(3) for at in starts], axis=0
    )
    weights = weight_ref[0].reshape(tiles * lanes, lanes)
    crossed = lax.dot_general(
        x.astype(bf16), weights, (((1,), (1,)), ((), ())), preferred_element_type=f32
    )
    line = lax.broadcasted_iota(jnp.int32, (tiles, lanes), 0)
    gap = jnp.zeros((tiles, lanes), f32)
    normals = []
    for c in range(3):
        interp = jnp.zeros((tiles, lanes), f32)
        for t in range(tiles):
            here = crossed[c * tiles : (c + 1) * tiles, t * lanes : (t + 1) * lanes]
            interp = jnp.where(line == t, here, interp)
        faces = [face_ref[0, t] for t in range(tiles)]
        normal = jnp.concatenate([normal_ref[0, c, pl.ds(f, 1)] for f in faces], axis=0)
        pos = jnp.concatenate([pos_ref[0, c, pl.ds(f, 1)] for f in faces], axis=0)
        gap += normal * (interp - pos)
        normals.append(normal)
    pressure = penalty * jnp.maximum(-gap, 0.0)
    push = [pressure * normal for normal in normals]
    spread = jnp.concatenate(
        [
            jnp.concatenate([jnp.where(line == t, p, 0.0) for p in push], axis=0).astype(bf16)
            for t in range(tiles)
        ],
        axis=1,
    )
    forces = jnp.dot(spread, weights, preferred_element_type=f32)
    for j in range(parts):
        out_ref[j] = forces


def list_kernel(cap, tiles, slots_ref, region_ref, list_ref, run_of):
    parts = slots_ref.shape[0]
    nblk = region_ref.shape[1]
    me = lax.axis_index("dom")
    for q in range(nblk // cap):
        run_of[region_ref[0, q * cap]] = q * cap

    def pick(j, filled):
        for t in range(tiles):
            slot = slots_ref[j, t]
            mine = slot // cap == me
            list_ref[0, filled] = j * 3 * tiles + t
            list_ref[1, filled] = jnp.where(mine, run_of[j] + slot % cap, 0)
            filled = filled + jnp.where(mine, 1, 0)
        return filled

    filled = lax.fori_loop(0, parts, pick, 0)
    for i in range(8):
        list_ref[0, filled + i] = 0
        list_ref[1, filled + i] = 0
    list_ref[0, list_ref.shape[1] - 1] = filled


def contact_kernel(
    tiles, list_ref, back_ref, surf_ref, part_ref, mass_ref, lo_ref, hi_ref, out_ref, share_lo_ref, share_hi_ref
):
    tops = mass_ref.shape[0] // 2
    out_ref[...] = part_ref[...]
    filled = list_ref[0, list_ref.shape[1] - 1]

    def spread(g, _):
        nodes, values = [], [[], [], []]
        for i in range(8):
            row = surf_ref[0, pl.ds(list_ref[1, g * 8 + i], 1)]
            nodes.append(jnp.where(g * 8 + i < filled, row, -1))
            for c in range(3):
                values[c].append(back_ref[pl.ds(list_ref[0, g * 8 + i] + c * tiles, 1)])
        sums = node_sums(nodes, values, tops)
        for c in range(3):
            add_halves(out_ref, sums, c, tops)
        return 0

    lax.fori_loop(0, (filled + 7) // 8, spread, 0)
    shared = lo_ref.shape[0]
    tables = [two_parts(halves(out_ref, c, tops)) for c in range(3)]
    tables.append(two_parts(halves(mass_ref, 0, tops)))
    values = lookup(tables, [ref[k : k + 1] for ref in (lo_ref, hi_ref) for k in range(shared)])
    for c in range(4):
        share_lo_ref[c * shared : (c + 1) * shared] = jnp.concatenate(values[c][:shared], axis=0)
        share_hi_ref[c * shared : (c + 1) * shared] = jnp.concatenate(values[c][shared:], axis=0)


def share_kernel(part_ref, mass_ref, up_ref, down_ref, lo_ref, hi_ref, out_ref, out_mass_ref):
    tops = mass_ref.shape[0] // 2
    out_ref[...] = part_ref[...]
    out_mass_ref[...] = mass_ref[...]
    shared = lo_ref.shape[0]
    nodes = [ref[k : k + 1] for ref in (hi_ref, lo_ref) for k in range(shared)]
    values = [
        [ref[c * shared + k : c * shared + k + 1] for ref in (up_ref, down_ref) for k in range(shared)]
        for c in range(4)
    ]
    sums = node_sums(nodes, values, tops)
    for c in range(3):
        add_halves(out_ref, sums, c, tops)
    add_halves(out_mass_ref, sums, 3, tops, 0)


def accel_kernel(mass_ref, *refs):
    sums, out_ref = refs[:-1], refs[-1]
    terms = [ref[...] for ref in sums]
    while len(terms) > 1:
        terms = [a + b for a, b in zip(terms[::2], terms[1::2])]
    size = mass_ref.shape[0]
    for c in range(3):
        at = slice(c * size, (c + 1) * size)
        out_ref[at] = terms[0][at] / mass_ref[...]


def shifted(block, axis, distance):
    devices = range(lax.axis_size(axis))
    route = [(i - distance, i) for i in devices if i - distance in devices]
    return lax.ppermute(block, axis, route)


def on_device(
    coords,
    disp,
    mass,
    stiffness,
    elem_nodes,
    modulus,
    surf_nodes,
    block_region,
    face_pos,
    face_normal,
    tile_slot,
    tile_face,
    tile_weight,
    shared_lo,
    shared_hi,
):
    parts = lax.axis_size("dom")
    mates = lax.axis_size("rep")
    nodes_all = disp.shape[2]
    nblk = surf_nodes.shape[1]
    tiles = tile_slot.shape[1]
    cap = max(2, 2 * nblk // parts)
    rows = (3 * cap + 1 + 15) // 16 * 16
    node_array = jax.ShapeDtypeStruct((3 * nodes_all // lanes, lanes), f32)
    mass_array = jax.ShapeDtypeStruct((nodes_all // lanes, lanes), f32)
    coords = coords.reshape(node_array.shape)
    disp = disp.reshape(node_array.shape)
    mass = mass.reshape(mass_array.shape)
    shared_lo = shared_lo.reshape(-1, lanes)
    shared_hi = shared_hi.reshape(-1, lanes)
    share = jax.ShapeDtypeStruct((4 * shared_lo.shape[0], lanes), f32)

    outgoing = call(
        functools.partial(pack_kernel, cap),
        jax.ShapeDtypeStruct((parts, rows, lanes), bf16),
        [smem, smem, vmem, vmem, vmem],
        vmem,
        [pltpu.VMEM((nblk // cap, rows, lanes), f32)],
        1 << 30,
    )(block_region, tile_slot, coords, disp, surf_nodes)
    arrived = lax.all_to_all(outgoing, "dom", split_axis=0, concat_axis=0, tiled=True)

    part = call(
        element_kernel,
        node_array,
        [vmem] * 4,
        vmem,
        [
            pltpu.VMEM((24, modulus.shape[1]), f32),
            pltpu.VMEM((3 * nodes_all // wide, wide), f32),
        ],
        1 << 32,
    )(disp, stiffness, modulus, elem_nodes)

    forces, slots = call(
        functools.partial(tile_kernel, cap),
        (
            jax.ShapeDtypeStruct((parts, 3 * tiles, lanes), f32),
            jax.ShapeDtypeStruct((parts, lanes), jnp.int32),
        ),
        [smem, smem] + [vmem] * 4 + [pl.BlockSpec(memory_space=pl.ANY)],
        (vmem, vmem),
        [pltpu.VMEM((parts * rows, lanes), f32)],
        1 << 28,
    )(
        tile_slot,
        tile_face,
        arrived,
        jnp.swapaxes(face_pos, 1, 2),
        jnp.swapaxes(face_normal, 1, 2),
        tile_weight,
        part,
    )
    back = lax.all_to_all(forces, "dom", split_axis=0, concat_axis=0, tiled=True)
    picks = call(
        functools.partial(list_kernel, cap, tiles),
        jax.ShapeDtypeStruct((2, parts * tiles + 16), jnp.int32),
        [smem, smem],
        smem,
        [pltpu.SMEM((parts,), jnp.int32)],
        1 << 24,
    )(slots, block_region)

    part, share_lo, share_hi = call(
        functools.partial(contact_kernel, tiles),
        (node_array, share, share),
        [smem] + [vmem] * 6,
        (vmem, vmem, vmem),
        [],
        1 << 28,
    )(picks, back.reshape(-1, lanes), surf_nodes, part, mass, shared_lo, shared_hi)
    from_upper = shifted(share_lo, "dom", -1)
    from_lower = shifted(share_hi, "dom", 1)

    own, own_mass = call(
        share_kernel, (node_array, mass_array), [vmem] * 6, (vmem, vmem), [], 1 << 28
    )(part, mass, from_upper, from_lower, shared_lo, shared_hi)
    others = [
        lax.ppermute(own, "rep", [(i, i ^ k) for i in range(mates)]) for k in range(1, mates)
    ]
    accel = call(accel_kernel, node_array, [vmem] * (2 + len(others)), vmem, [], 1 << 24)(
        own_mass, own, *others
    )
    return accel.reshape(1, 3, nodes_all)


def solution(mesh):
    in_specs = (
        P("dom", None, None),
        P("dom", None, None),
        P("dom", None),
        P(),
        P("dom", None, "rep"),
        P("dom", "rep"),
        P("dom", None, None),
        P("dom", None),
        P("dom", None, None, None),
        P("dom", None, None, None),
        P("dom", "rep"),
        P("dom", "rep"),
        P("dom", "rep", None, None),
        P("dom", None),
        P("dom", None),
    )
    out_specs = P("dom", None, None)
    return jax.shard_map(
        on_device, mesh=mesh, in_specs=in_specs, out_specs=out_specs, check_vma=False
    )
```

profile of v0, /device:TPU:9, one launch (start us, length us, event | category | flops | bytes accessed | tf_op | source)
XLA Modules:
  0.0 53.8 jit_solution(4580879641256732295)
XLA Ops:
  0.0 0.7 %copy-done.14 = s32[1,8]{1,0:T(1,128)S(1)} copy-done((s32[1,8]{1,0:T(1,128)S(1)}, s32[1,8]{1,0:T(1,128)}, u32[]{:S(2)}) %copy-start.14) | copy-done | bytes 56
  0.7 0.0 copy-done.16
  0.7 0.9 %copy-done.1 = f32[1,3,8192]{2,0,1:T(1,128)S(1)} copy-done((f32[1,3,8192]{2,0,1:T(1,128)S(1)}, f32[1,3,8192]{2,0,1:T(1,128)}, u32[]{:S(2)}) %copy-start.1) | copy-done | bytes 98328
  1.6 0.9 %copy-done.2 = f32[1,3,8192]{2,0,1:T(1,128)S(1)} copy-done((f32[1,3,8192]{2,0,1:T(1,128)S(1)}, f32[1,3,8192]{2,0,1:T(1,128)}, u32[]{:S(2)}) %copy-start.2) | copy-done | bytes 98328
  2.5 0.8 %copy-done.6 = s32[1,128,128]{2,1,0:T(8,128)S(1)} copy-done((s32[1,128,128]{2,1,0:T(8,128)S(1)}, s32[1,128,128]{2,1,0:T(8,128)}, u32[]{:S(2)}) %copy-start.6) | copy-done | bytes 65560
  3.3 3.9 %shard_map.145 = bf16[8,112,128]{2,1,0:T(8,128)(2,1)} custom-call(s32[1,128]{1,0:T(1,128)S(1)} %copy-done.16, s32[1,8]{1,0:T(1,128)S(1)} %copy-done.14, f32[192,128]{1,0:T(8,128)S(1)} %bitcast.10, f32[192,128]{1,0:T(8,128)S(1)} %bitcast.11, s32[1,128,128]{2,1,0:T(8,128)S(1)} %copy-done.6), custom_call_target="tpu_custom_call" | custom-call | flops 1073741824 | bytes 1048576 | tf_op jit(solution)/shard_map/pallas_call | solution.py:319
  7.2 5.9 %all-to-all-start = ((bf16[8,112,128]{2,1,0:T(8,128)(2,1)}), bf16[8,112,128]{2,1,0:T(8,128)(2,1)S(1)}, u32[]{:S(2)}, u32[]{:S(2)}) async-start(bf16[8,112,128]{2,1,0:T(8,128)(2,1)} %shard_map.145), calls=%async_computation | async-start | bytes 458752 | tf_op jit(solution)/shard_map/all_to_all | solution.py:327
  13.1 0.0 copy-done.8
  13.1 0.0 copy-start
  13.1 0.0 copy-start.4
  13.1 0.0 copy-start.5
  13.1 3.5 %shard_map.146.after_ref.part_ref = f32[192,128]{1,0:T(8,128)S(1)} custom-call(f32[192,128]{1,0:T(8,128)S(1)} %bitcast.12, f32[24,24]{1,0:T(8,128)S(1)} %copy-done.10, f32[1,1024]{1,0:T(1,128)S(1)} %copy-done.11, s32[1,8,1024]{2,1,0:T(8,128)S(1)} %copy-done.8), custom_call_target="tpu_custom_call" | custom-call | flops 4294967296 | bytes 1048576 | tf_op jit(solution)/shard_map/pallas_call | solution.py:329
  16.7 2.1 %all-to-all-done.got_ref = bf16[8,112,128]{2,1,0:T(8,128)(2,1)S(1)} async-done(((bf16[8,112,128]{2,1,0:T(8,128)(2,1)}), bf16[8,112,128]{2,1,0:T(8,128)(2,1)S(1)}, u32[]{:S(2)}, u32[]{:S(2)}) %all-to-all-start) | async-done | bytes 229408 | tf_op jit(solution)/shard_map/all_to_all | solution.py:327
  18.8 0.6 %copy-done.15 = s32[1,8]{1,0:T(1,128)S(1)} copy-done((s32[1,8]{1,0:T(1,128)S(1)}, s32[1,8]{1,0:T(1,128)}, u32[]{:S(2)}) %copy-start.15) | copy-done | bytes 56
  19.5 1.6 %shard_map.147 = (f32[8,24,128]{2,1,0:T(8,128)}, s32[8,128]{1,0:T(8,128)S(1)}) custom-call(s32[1,8]{1,0:T(1,128)S(1)} %copy-done.14, s32[1,8]{1,0:T(1,128)S(1)} %copy-done.15, bf16[8,112,128]{2,1,0:T(8,128)(2,1)S(1)} %all-to-all-done.got_ref, f32[1,3,64,128]{3,2,1,0:T(8,128)S(1)} %bitcast.13, f32[1,3,64,128]{3,2,1,0:T(8,128)S(1)} %bitcast.14, ...), custom_call_target="tpu_custom_call" | custom-call | flops 268435456 | bytes 1048576 | tf_op jit(solution)/shard_map/pallas_call | solution.py:341
  21.1 5.9 %all-to-all-start.1 = ((f32[8,24,128]{2,1,0:T(8,128)}), f32[8,24,128]{2,1,0:T(8,128)S(1)}, u32[]{:S(2)}, u32[]{:S(2)}) async-start(f32[8,24,128]{2,1,0:T(8,128)} %get-tuple-element.13), calls=%async_computation.1 | async-start | bytes 196608 | tf_op jit(solution)/shard_map/all_to_all | solution.py:360
  26.9 1.9 %shard_map.148.list_ref = s32[2,80]{1,0:T(2,128)S(1)} custom-call(s32[8,128]{1,0:T(8,128)S(1)} %get-tuple-element.12.slots_ref, s32[1,128]{1,0:T(1,128)S(1)} %copy-done.16), custom_call_target="tpu_custom_call" | custom-call | flops 16777216 | bytes 1048576 | tf_op jit(solution)/shard_map/pallas_call | solution.py:361
  28.8 2.4 %all-to-all-done.1 = f32[8,24,128]{2,1,0:T(8,128)S(1)} async-done(((f32[8,24,128]{2,1,0:T(8,128)}), f32[8,24,128]{2,1,0:T(8,128)S(1)}, u32[]{:S(2)}, u32[]{:S(2)}) %all-to-all-start.1) | async-done | bytes 98336 | tf_op jit(solution)/shard_map/all_to_all | solution.py:360
  31.3 0.7 %copy-done.12 = s32[1,512]{1,0:T(1,128)S(1)} copy-done((s32[1,512]{1,0:T(1,128)S(1)}, s32[1,512]{1,0:T(1,128)}, u32[]{:S(2)}) %copy-start.12) | copy-done | bytes 2072
  31.9 1.6 %shard_map.149 = (f32[192,128]{1,0:T(8,128)S(1)}, f32[16,128]{1,0:T(8,128)S(1)}, f32[16,128]{1,0:T(8,128)S(1)}) custom-call(s32[2,80]{1,0:T(2,128)S(1)} %shard_map.148.list_ref, f32[192,128]{1,0:T(8,128)S(1)} %bitcast.9, s32[1,128,128]{2,1,0:T(8,128)S(1)} %copy-done.7, f32[192,128]{1,0:T(8,128)S(1)} %shard_map.146.after_ref.part_ref, ...), custom_call_target="tpu_custom_call" | custom-call | flops 268435456 | bytes 1048576 | tf_op jit(solution)/shard_map/pallas_call | solution.py:370
  33.6 2.9 %collective-permute-start = (f32[16,128]{1,0:T(8,128)S(1)}, f32[16,128]{1,0:T(8,128)S(1)}, u32[]{:S(2)}, u32[]{:S(2)}) collective-permute-start(f32[16,128]{1,0:T(8,128)S(1)} %get-tuple-element.15), channel_id=1, source_target_pairs={{4,0},{8,4},{12,8},{16,12},{20,16},{24,20},{28,24},{5,1},{9,5},{13... | collective-permute-start | bytes 24584 | tf_op jit(solution)/shard_map/ppermute | solution.py:283
  36.5 2.3 %collective-permute-start.1 = (f32[16,128]{1,0:T(8,128)S(1)}, f32[16,128]{1,0:T(8,128)S(1)}, u32[]{:S(2)}, u32[]{:S(2)}) collective-permute-start(f32[16,128]{1,0:T(8,128)S(1)} %get-tuple-element.16), channel_id=1, source_target_pairs={{0,4},{4,8},{8,12},{12,16},{16,20},{20,24},{24,28},{1,5},{5,9},{9,... | collective-permute-start | bytes 24584 | tf_op jit(solution)/shard_map/ppermute | solution.py:283
  38.9 0.0 collective-permute-done.up_ref
  38.9 2.9 %collective-permute-done.1.down_ref = f32[16,128]{1,0:T(8,128)S(1)} collective-permute-done((f32[16,128]{1,0:T(8,128)S(1)}, f32[16,128]{1,0:T(8,128)S(1)}, u32[]{:S(2)}, u32[]{:S(2)}) %collective-permute-start.1) | collective-permute-done | bytes 8224 | tf_op jit(solution)/shard_map/ppermute | solution.py:283
  41.8 0.4 shard_map.150
  42.2 4.3 %collective-permute-start.2 = (f32[192,128]{1,0:T(8,128)S(1)}, f32[192,128]{1,0:T(8,128)S(1)}, u32[]{:S(2)}, u32[]{:S(2)}) collective-permute-start(f32[192,128]{1,0:T(8,128)S(1)} %get-tuple-element.18.refs_0_), channel_id=1, source_target_pairs={{0,1},{1,0},{2,3},{3,2},{4,5},{5,4},{6,7},{7,6},{8,9},{9,8},{10,11... | collective-permute-start | bytes 294920 | tf_op jit(solution)/shard_map/ppermute | solution.py:385
  46.5 0.9 %collective-permute-start.3 = (f32[192,128]{1,0:T(8,128)S(1)}, f32[192,128]{1,0:T(8,128)S(1)}, u32[]{:S(2)}, u32[]{:S(2)}) collective-permute-start(f32[192,128]{1,0:T(8,128)S(1)} %get-tuple-element.18.refs_0_), channel_id=1, source_target_pairs={{0,2},{1,3},{2,0},{3,1},{4,6},{5,7},{6,4},{7,5},{8,10},{9,11},{10,... | collective-permute-start | bytes 294920 | tf_op jit(solution)/shard_map/ppermute | solution.py:385
  47.3 0.9 %collective-permute-start.4 = (f32[192,128]{1,0:T(8,128)S(1)}, f32[192,128]{1,0:T(8,128)S(1)}, u32[]{:S(2)}, u32[]{:S(2)}) collective-permute-start(f32[192,128]{1,0:T(8,128)S(1)} %get-tuple-element.18.refs_0_), channel_id=1, source_target_pairs={{0,3},{1,2},{2,1},{3,0},{4,7},{5,6},{6,5},{7,4},{8,11},{9,10},{10,... | collective-permute-start | bytes 294920 | tf_op jit(solution)/shard_map/ppermute | solution.py:385
  48.2 0.0 collective-permute-done.2.refs_1_
  48.2 2.7 %collective-permute-done.3.refs_2_ = f32[192,128]{1,0:T(8,128)S(1)} collective-permute-done((f32[192,128]{1,0:T(8,128)S(1)}, f32[192,128]{1,0:T(8,128)S(1)}, u32[]{:S(2)}, u32[]{:S(2)}) %collective-permute-start.3) | collective-permute-done | bytes 98336 | tf_op jit(solution)/shard_map/ppermute | solution.py:385
  50.8 2.3 %collective-permute-done.4.refs_3_ = f32[192,128]{1,0:T(8,128)S(1)} collective-permute-done((f32[192,128]{1,0:T(8,128)S(1)}, f32[192,128]{1,0:T(8,128)S(1)}, u32[]{:S(2)}, u32[]{:S(2)}) %collective-permute-start.4) | collective-permute-done | bytes 98336 | tf_op jit(solution)/shard_map/ppermute | solution.py:385
  53.1 0.7 %shard_map.151 = f32[192,128]{1,0:T(8,128)} custom-call(f32[64,128]{1,0:T(8,128)S(1)} %get-tuple-element.17.mass_ref, f32[192,128]{1,0:T(8,128)S(1)} %get-tuple-element.18.refs_0_, f32[192,128]{1,0:T(8,128)S(1)} %collective-permute-done.2.refs_1_, f32[192,128]{1,0:T(8,128)S(1)} %collective-permute-done.3.refs_2_, f32[192,128]{1,0:T(8,128)S(1)} %collective-permute-done.4.refs_3_), custom_call_target="tpu_custom_call" | custom-call | flops 16777216 | bytes 1048576 | tf_op jit(solution)/shard_map/pallas_call | solution.py:387
  (23 shorter events, 0.0 us)
Async XLA Ops:
  0.0 0.7 %copy-start.14 = (s32[1,8]{1,0:T(1,128)S(1)}, s32[1,8]{1,0:T(1,128)}, u32[]{:S(2)}) copy-start(s32[1,8]{1,0:T(1,128)} %slot_ref.3) | copy-start | bytes 100
  0.0 0.7 %copy-start.16 = (s32[1,128]{1,0:T(1,128)S(1)}, s32[1,128]{1,0:T(1,128)}, u32[]{:S(2)}) copy-start(s32[1,128]{1,0:T(1,128)} %region_ref.3) | copy-start | bytes 1540
  0.7 0.9 %copy-start.1 = (f32[1,3,8192]{2,0,1:T(1,128)S(1)}, f32[1,3,8192]{2,0,1:T(1,128)}, u32[]{:S(2)}) copy-start(f32[1,3,8192]{2,0,1:T(1,128)} %param.15) | copy-start | bytes 294916
  1.6 0.9 %copy-start.2 = (f32[1,3,8192]{2,0,1:T(1,128)S(1)}, f32[1,3,8192]{2,0,1:T(1,128)}, u32[]{:S(2)}) copy-start(f32[1,3,8192]{2,0,1:T(1,128)} %param.16) | copy-start | bytes 294916
  2.5 0.8 %copy-start.6 = (s32[1,128,128]{2,1,0:T(8,128)S(1)}, s32[1,128,128]{2,1,0:T(8,128)}, u32[]{:S(2)}) copy-start(s32[1,128,128]{2,1,0:T(8,128)} %surf_ref.3) | copy-start | bytes 196612
  7.2 5.9 %copy-start.3 = (f32[1,3,8192]{2,0,1:T(1,128)S(1)}, f32[1,3,8192]{2,0,1:T(1,128)}, u32[]{:S(2)}) copy-start(f32[1,3,8192]{2,0,1:T(1,128)} %param.16) | copy-start | bytes 294916
  7.2 5.9 %copy-start.8 = (s32[1,8,1024]{2,1,0:T(8,128)S(1)}, s32[1,8,1024]{2,1,0:T(8,128)}, u32[]{:S(2)}) copy-start(s32[1,8,1024]{2,1,0:T(8,128)} %nodes_ref.1) | copy-start | bytes 98308
  7.2 5.9 %copy-start.10 = (f32[24,24]{1,0:T(8,128)S(1)}, f32[24,24]{1,0:T(8,128)}, u32[]{:S(2)}) copy-start(f32[24,24]{1,0:T(8,128)} %stiff_ref.1) | copy-start | bytes 6916
  7.2 5.9 %copy-start.11 = (f32[1,1024]{1,0:T(1,128)S(1)}, f32[1,1024]{1,0:T(1,128)}, u32[]{:S(2)}) copy-start(f32[1,1024]{1,0:T(1,128)} %modulus_ref.1) | copy-start | bytes 12292
  7.2 11.6 %all-to-all-start = ((bf16[8,112,128]{2,1,0:T(8,128)(2,1)}), bf16[8,112,128]{2,1,0:T(8,128)(2,1)S(1)}, u32[]{:S(2)}, u32[]{:S(2)}) async-start(bf16[8,112,128]{2,1,0:T(8,128)(2,1)} %shard_map.145), calls=%async_computation | async-start | bytes 458752 | tf_op jit(solution)/shard_map/all_to_all | solution.py:327
  13.1 5.7 %copy-start = (bf16[1,8,128,128]{3,2,1,0:T(8,128)(2,1)S(1)}, bf16[1,8,128,128]{3,2,1,0:T(8,128)(2,1)}, u32[]{:S(2)}) copy-start(bf16[1,8,128,128]{3,2,1,0:T(8,128)(2,1)} %weight_ref.1) | copy-start | bytes 786436
  13.1 5.7 %copy-start.4 = (f32[1,64,3,128]{3,1,2,0:T(8,128)S(1)}, f32[1,64,3,128]{3,1,2,0:T(8,128)}, u32[]{:S(2)}) copy-start(f32[1,64,3,128]{3,1,2,0:T(8,128)} %param.23) | copy-start | bytes 294916
  13.1 5.7 %copy-start.5 = (f32[1,64,3,128]{3,1,2,0:T(8,128)S(1)}, f32[1,64,3,128]{3,1,2,0:T(8,128)}, u32[]{:S(2)}) copy-start(f32[1,64,3,128]{3,1,2,0:T(8,128)} %param.24) | copy-start | bytes 294916
  18.8 0.7 %copy-start.15 = (s32[1,8]{1,0:T(1,128)S(1)}, s32[1,8]{1,0:T(1,128)}, u32[]{:S(2)}) copy-start(s32[1,8]{1,0:T(1,128)} %face_ref.1) | copy-start | bytes 100
  19.5 11.8 %copy-start.9 = (f32[1,8192]{1,0:T(1,128)S(1)}, f32[1,8192]{1,0:T(1,128)}, u32[]{:S(2)}) copy-start(f32[1,8192]{1,0:T(1,128)} %param.17) | copy-start | bytes 98308
  21.1 10.2 %copy-start.13 = (s32[1,512]{1,0:T(1,128)S(1)}, s32[1,512]{1,0:T(1,128)}, u32[]{:S(2)}) copy-start(s32[1,512]{1,0:T(1,128)} %param.29) | copy-start | bytes 6148
  21.1 10.2 %all-to-all-start.1 = ((f32[8,24,128]{2,1,0:T(8,128)}), f32[8,24,128]{2,1,0:T(8,128)S(1)}, u32[]{:S(2)}, u32[]{:S(2)}) async-start(f32[8,24,128]{2,1,0:T(8,128)} %get-tuple-element.13), calls=%async_computation.1 | async-start | bytes 196608 | tf_op jit(solution)/shard_map/all_to_all | solution.py:360
  26.9 4.3 %copy-start.7 = (s32[1,128,128]{2,1,0:T(8,128)S(1)}, s32[1,128,128]{2,1,0:T(8,128)}, u32[]{:S(2)}) copy-start(s32[1,128,128]{2,1,0:T(8,128)} %surf_ref.3) | copy-start | bytes 196612
  31.3 0.7 %copy-start.12 = (s32[1,512]{1,0:T(1,128)S(1)}, s32[1,512]{1,0:T(1,128)}, u32[]{:S(2)}) copy-start(s32[1,512]{1,0:T(1,128)} %param.28) | copy-start | bytes 6148
  33.6 5.3 %collective-permute-start = (f32[16,128]{1,0:T(8,128)S(1)}, f32[16,128]{1,0:T(8,128)S(1)}, u32[]{:S(2)}, u32[]{:S(2)}) collective-permute-start(f32[16,128]{1,0:T(8,128)S(1)} %get-tuple-element.15), channel_id=1, source_target_pairs={{4,0},{8,4},{12,8},{16,12},{20,16},{24,20},{28,24},{5,1},{9,5},{13... | collective-permute-start | bytes 24584 | tf_op jit(solution)/shard_map/ppermute | solution.py:283
  36.5 5.3 %collective-permute-start.1 = (f32[16,128]{1,0:T(8,128)S(1)}, f32[16,128]{1,0:T(8,128)S(1)}, u32[]{:S(2)}, u32[]{:S(2)}) collective-permute-start(f32[16,128]{1,0:T(8,128)S(1)} %get-tuple-element.16), channel_id=1, source_target_pairs={{0,4},{4,8},{8,12},{12,16},{16,20},{20,24},{24,28},{1,5},{5,9},{9,... | collective-permute-start | bytes 24584 | tf_op jit(solution)/shard_map/ppermute | solution.py:283
  42.2 6.0 %collective-permute-start.2 = (f32[192,128]{1,0:T(8,128)S(1)}, f32[192,128]{1,0:T(8,128)S(1)}, u32[]{:S(2)}, u32[]{:S(2)}) collective-permute-start(f32[192,128]{1,0:T(8,128)S(1)} %get-tuple-element.18.refs_0_), channel_id=1, source_target_pairs={{0,1},{1,0},{2,3},{3,2},{4,5},{5,4},{6,7},{7,6},{8,9},{9,8},{10,11... | collective-permute-start | bytes 294920 | tf_op jit(solution)/shard_map/ppermute | solution.py:385
  46.5 4.4 %collective-permute-start.3 = (f32[192,128]{1,0:T(8,128)S(1)}, f32[192,128]{1,0:T(8,128)S(1)}, u32[]{:S(2)}, u32[]{:S(2)}) collective-permute-start(f32[192,128]{1,0:T(8,128)S(1)} %get-tuple-element.18.refs_0_), channel_id=1, source_target_pairs={{0,2},{1,3},{2,0},{3,1},{4,6},{5,7},{6,4},{7,5},{8,10},{9,11},{10,... | collective-permute-start | bytes 294920 | tf_op jit(solution)/shard_map/ppermute | solution.py:385
  47.3 5.8 %collective-permute-start.4 = (f32[192,128]{1,0:T(8,128)S(1)}, f32[192,128]{1,0:T(8,128)S(1)}, u32[]{:S(2)}, u32[]{:S(2)}) collective-permute-start(f32[192,128]{1,0:T(8,128)S(1)} %get-tuple-element.18.refs_0_), channel_id=1, source_target_pairs={{0,3},{1,2},{2,1},{3,0},{4,7},{5,6},{6,5},{7,4},{8,11},{9,10},{10,... | collective-permute-start | bytes 294920 | tf_op jit(solution)/shard_map/ppermute | solution.py:385
where the time goes:
time: 54.3 us; the launch traced here: 53.8 us
  starting transfers between devices  23 us (42%)
  Pallas kernels  13.5 us (25%)
  waiting for transfers between devices  12.4 us (23%)
  local copies, waits for them, and re-layouts  4.65 us (9%)
    ppermute x3, starting transfers between devices, on_device(): lax.ppermute(own, 'rep', [(i, i ^ k) for i in range(mates)])  5.99 us
    all_to_all x1, starting transfers between devices, on_device(): lax.all_to_all(forces, 'dom', split_axis=0, concat_axis=0, tiled=True)  5.88 us
    all_to_all x1, starting transfers between devices, on_device(): lax.all_to_all(outgoing, 'dom', split_axis=0, concat_axis=0, tiled=True)  5.86 us
    ppermute x2, starting transfers between devices, shifted(): return lax.ppermute(block, axis, route)  5.28 us
    ppermute x3, waiting for transfers between devices, on_device(): lax.ppermute(own, 'rep', [(i, i ^ k) for i in range(mates)])  4.93 us
    unnamed x34, local copies, waits for them, and re-layouts  4.65 us
    pallas_call x1, Pallas kernels, on_device(): call(functools.partial(pack_kernel, cap), jax.ShapeDtypeStruct((parts, ro...  3.9 us
    pallas_call x1, Pallas kernels, on_device(): call(element_kernel, node_array, [vmem] * 4, vmem, [pltpu.VMEM((24, modul...  3.53 us
  transfers between devices with their start and end apart: 7, of which 5 were waited for; matrix products, arithmetic and copies ran while one was open for 0% of the time, Pallas kernels for 10%

commit v1 on v0

--- a/solution.py
+++ b/solution.py
@@ -12,18 +12,19 @@
 wide = 256
 vmem = pl.BlockSpec(memory_space=pltpu.VMEM)
 smem = pl.BlockSpec(memory_space=pltpu.SMEM)
+hbm = pl.BlockSpec(memory_space=pltpu.HBM)
 f32 = jnp.float32
 bf16 = jnp.bfloat16
 
 
-def call(body, out_shape, in_specs, out_specs, scratch, flops):
+def call(body, out_shape, in_specs, out_specs, scratch, flops, vmem_mib=32):
     return pl.pallas_call(
         body,
         out_shape=out_shape,
         in_specs=in_specs,
         out_specs=out_specs,
         scratch_shapes=scratch,
-        compiler_params=pltpu.CompilerParams(vmem_limit_bytes=32 * 1024 * 1024),
+        compiler_params=pltpu.CompilerParams(vmem_limit_bytes=vmem_mib * 1024 * 1024),
         cost_estimate=pl.CostEstimate(flops=flops, bytes_accessed=1 << 20, transcendentals=0),
     )
 
@@ -95,11 +96,23 @@
         ]
 
 
-def pack_kernel(cap, region_ref, slot_ref, coords_ref, disp_ref, surf_ref, out_ref, stage):
+def pack_kernel(
+    cap, region_hbm, slot_hbm, coords_hbm, disp_hbm, surf_hbm, out_ref,
+    stage, region_ref, slot_ref, coords_ref, disp_ref, surf_ref, sems,
+):
+    sources = (coords_hbm, disp_hbm, slot_hbm, surf_hbm, region_hbm)
+    places = (coords_ref, disp_ref, slot_ref, surf_ref, region_ref)
+    copies = [
+        pltpu.make_async_copy(a, b, sems.at[i]) for i, (a, b) in enumerate(zip(sources, places))
+    ]
+    for copy in copies:
+        copy.start()
     parts, rows, _ = out_ref.shape
     nblk = surf_ref.shape[1]
     tiles = slot_ref.shape[1]
     tops = coords_ref.shape[0] // 6
+    for copy in copies:
+        copy.wait()
     rest = (rows - 3 * cap, lanes)
     lane = lax.broadcasted_iota(jnp.int32, rest, 1)
     line = lax.broadcasted_iota(jnp.int32, rest, 0)
@@ -127,7 +140,17 @@
         out_ref[region_ref[0, q * cap]] = stage[q].astype(bf16)
 
 
-def element_kernel(disp_ref, stiff_ref, modulus_ref, nodes_ref, out_ref, local, sums):
+def element_kernel(
+    cap, rows, slot_ref, face_ref, pos_ref, normal_ref, disp_ref, stiff_ref, modulus_ref, nodes_ref,
+    out_ref, faces_ref, starts_ref, local, sums,
+):
+    tiles = slot_ref.shape[1]
+    for t in range(tiles):
+        starts_ref[0, t] = (slot_ref[0, t] // cap) * rows + slot_ref[0, t] % cap
+        for c in range(3):
+            at = c * tiles + t
+            faces_ref[0, at : at + 1] = pos_ref[0, c, pl.ds(face_ref[0, t], 1)]
+            faces_ref[1, at : at + 1] = normal_ref[0, c, pl.ds(face_ref[0, t], 1)]
     corners, count = nodes_ref.shape[1:]
     tops = disp_ref.shape[0] // 6
     tables = [two_parts(halves(disp_ref, c, tops)) for c in range(3)]
@@ -153,19 +176,16 @@
         add_halves(out_ref, sums[...], c, tops)
 
 
-def tile_kernel(
-    cap, slot_ref, face_ref, got_ref, pos_ref, normal_ref, weight_ref, after_ref, out_ref, slots_ref, flat
-):
+def tile_kernel(cap, starts_ref, got_ref, faces_ref, weight_ref, out_ref, slots_ref, flat):
     parts, rows, _ = got_ref.shape
-    tiles = slot_ref.shape[1]
+    tiles = starts_ref.shape[1]
     for j in range(parts):
         flat[j * rows : (j + 1) * rows] = got_ref[j].astype(f32)
     slots_ref[...] = jnp.concatenate(
         [flat[j * rows + 3 * cap : j * rows + 3 * cap + 1] for j in range(parts)], axis=0
     ).astype(jnp.int32)
-    starts = [(slot_ref[0, t] // cap) * rows + slot_ref[0, t] % cap for t in range(tiles)]
     x = jnp.concatenate(
-        [flat[pl.ds(at + c * cap, 1)] for c in range(3) for at in starts], axis=0
+        [flat[pl.ds(starts_ref[0, t] + c * cap, 1)] for c in range(3) for t in range(tiles)], axis=0
     )
     weights = weight_ref[0].reshape(tiles * lanes, lanes)
     crossed = lax.dot_general(
@@ -179,10 +199,8 @@
         for t in range(tiles):
             here = crossed[c * tiles : (c + 1) * tiles, t * lanes : (t + 1) * lanes]
             interp = jnp.where(line == t, here, interp)
-        faces = [face_ref[0, t] for t in range(tiles)]
-        normal = jnp.concatenate([normal_ref[0, c, pl.ds(f, 1)] for f in faces], axis=0)
-        pos = jnp.concatenate([pos_ref[0, c, pl.ds(f, 1)] for f in faces], axis=0)
-        gap += normal * (interp - pos)
+        normal = faces_ref[1, c * tiles : (c + 1) * tiles]
+        gap += normal * (interp - faces_ref[0, c * tiles : (c + 1) * tiles])
         normals.append(normal)
     pressure = penalty * jnp.maximum(-gap, 0.0)
     push = [pressure * normal for normal in normals]
@@ -198,7 +216,10 @@
         out_ref[j] = forces
 
 
-def list_kernel(cap, tiles, slots_ref, region_ref, list_ref, run_of):
+def list_kernel(cap, tiles, slots_ref, region_ref, lo_ref, hi_ref, list_ref, both_ref, run_of):
+    shared = lo_ref.shape[0]
+    both_ref[:shared] = lo_ref[...]
+    both_ref[shared:] = hi_ref[...]
     parts = slots_ref.shape[0]
     nblk = region_ref.shape[1]
     me = lax.axis_index("dom")
@@ -221,10 +242,8 @@
     list_ref[0, list_ref.shape[1] - 1] = filled
 
 
-def contact_kernel(
-    tiles, list_ref, back_ref, surf_ref, part_ref, mass_ref, lo_ref, hi_ref, out_ref, share_lo_ref, share_hi_ref
-):
-    tops = mass_ref.shape[0] // 2
+def contact_kernel(tiles, list_ref, back_ref, surf_ref, part_ref, out_ref):
+    tops = part_ref.shape[0] // 6
     out_ref[...] = part_ref[...]
     filled = list_ref[0, list_ref.shape[1] - 1]
 
@@ -241,23 +260,30 @@
         return 0
 
     lax.fori_loop(0, (filled + 7) // 8, spread, 0)
-    shared = lo_ref.shape[0]
+
+
+def pair_kernel(part_ref, other_ref, mass_ref, both_ref, out_ref, share_lo_ref, share_hi_ref):
+    tops = mass_ref.shape[0] // 2
+    out_ref[...] = part_ref[...] + other_ref[...]
+    count = both_ref.shape[0]
+    shared = count // 2
     tables = [two_parts(halves(out_ref, c, tops)) for c in range(3)]
     tables.append(two_parts(halves(mass_ref, 0, tops)))
-    values = lookup(tables, [ref[k : k + 1] for ref in (lo_ref, hi_ref) for k in range(shared)])
+    values = lookup(tables, [both_ref[k : k + 1] for k in range(count)])
     for c in range(4):
         share_lo_ref[c * shared : (c + 1) * shared] = jnp.concatenate(values[c][:shared], axis=0)
         share_hi_ref[c * shared : (c + 1) * shared] = jnp.concatenate(values[c][shared:], axis=0)
 
 
-def share_kernel(part_ref, mass_ref, up_ref, down_ref, lo_ref, hi_ref, out_ref, out_mass_ref):
+def share_kernel(part_ref, mass_ref, up_ref, down_ref, both_ref, out_ref, out_mass_ref):
     tops = mass_ref.shape[0] // 2
     out_ref[...] = part_ref[...]
     out_mass_ref[...] = mass_ref[...]
-    shared = lo_ref.shape[0]
-    nodes = [ref[k : k + 1] for ref in (hi_ref, lo_ref) for k in range(shared)]
+    count = both_ref.shape[0]
+    shared = count // 2
+    nodes = [both_ref[k : k + 1] for k in range(count)]
     values = [
-        [ref[c * shared + k : c * shared + k + 1] for ref in (up_ref, down_ref) for k in range(shared)]
+        [ref[c * shared + k : c * shared + k + 1] for ref in (down_ref, up_ref) for k in range(shared)]
         for c in range(4)
     ]
     sums = node_sums(nodes, values, tops)
@@ -266,21 +292,24 @@
     add_halves(out_mass_ref, sums, 3, tops, 0)
 
 
-def accel_kernel(mass_ref, *refs):
-    sums, out_ref = refs[:-1], refs[-1]
-    terms = [ref[...] for ref in sums]
-    while len(terms) > 1:
-        terms = [a + b for a, b in zip(terms[::2], terms[1::2])]
+def accel_kernel(mass_ref, own_ref, other_ref, out_ref):
+    total = own_ref[...] + other_ref[...]
     size = mass_ref.shape[0]
     for c in range(3):
         at = slice(c * size, (c + 1) * size)
-        out_ref[at] = terms[0][at] / mass_ref[...]
+        out_ref[at] = total[at] / mass_ref[...]
 
 
 def shifted(block, axis, distance):
     devices = range(lax.axis_size(axis))
     route = [(i - distance, i) for i in devices if i - distance in devices]
     return lax.ppermute(block, axis, route)
+
+
+def from_mate(block, distance):
+    return lax.ppermute(
+        block, "rep", [(i, i ^ distance) for i in range(lax.axis_size("rep"))]
+    )
 
 
 def on_device(
@@ -319,24 +348,46 @@
     outgoing = call(
         functools.partial(pack_kernel, cap),
         jax.ShapeDtypeStruct((parts, rows, lanes), bf16),
-        [smem, smem, vmem, vmem, vmem],
+        [hbm] * 5,
         vmem,
-        [pltpu.VMEM((nblk // cap, rows, lanes), f32)],
+        [
+            pltpu.VMEM((nblk // cap, rows, lanes), f32),
+            pltpu.SMEM(block_region.shape, jnp.int32),
+            pltpu.SMEM(tile_slot.shape, jnp.int32),
+            pltpu.VMEM(coords.shape, f32),
+            pltpu.VMEM(disp.shape, f32),
+            pltpu.VMEM(surf_nodes.shape, jnp.int32),
+            pltpu.SemaphoreType.DMA((5,)),
+        ],
         1 << 30,
+        60,
     )(block_region, tile_slot, coords, disp, surf_nodes)
     arrived = lax.all_to_all(outgoing, "dom", split_axis=0, concat_axis=0, tiled=True)
 
-    part = call(
-        element_kernel,
-        node_array,
-        [vmem] * 4,
-        vmem,
+    part, faces, starts = call(
+        functools.partial(element_kernel, cap, rows),
+        (
+            node_array,
+            jax.ShapeDtypeStruct((2, 3 * tiles, lanes), f32),
+            jax.ShapeDtypeStruct((1, tiles), jnp.int32),
+        ),
+        [smem] * 2 + [vmem] * 6,
+        (vmem, vmem, smem),
         [
             pltpu.VMEM((24, modulus.shape[1]), f32),
             pltpu.VMEM((3 * nodes_all // wide, wide), f32),
         ],
         1 << 32,
-    )(disp, stiffness, modulus, elem_nodes)
+    )(
+        tile_slot,
+        tile_face,
+        jnp.swapaxes(face_pos, 1, 2),
+        jnp.swapaxes(face_normal, 1, 2),
+        disp,
+        stiffness,
+        modulus,
+        elem_nodes,
+    )
 
     forces, slots = call(
         functools.partial(tile_kernel, cap),
@@ -344,48 +395,40 @@
             jax.ShapeDtypeStruct((parts, 3 * tiles, lanes), f32),
             jax.ShapeDtypeStruct((parts, lanes), jnp.int32),
         ),
-        [smem, smem] + [vmem] * 4 + [pl.BlockSpec(memory_space=pl.ANY)],
+        [smem] + [vmem] * 3,
         (vmem, vmem),
         [pltpu.VMEM((parts * rows, lanes), f32)],
         1 << 28,
-    )(
-        tile_slot,
-        tile_face,
-        arrived,
-        jnp.swapaxes(face_pos, 1, 2),
-        jnp.swapaxes(face_normal, 1, 2),
-        tile_weight,
-        part,
-    )
+    )(starts, arrived, faces, tile_weight)
     back = lax.all_to_all(forces, "dom", split_axis=0, concat_axis=0, tiled=True)
-    picks = call(
+    both_array = jax.ShapeDtypeStruct((2 * shared_lo.shape[0], lanes), jnp.int32)
+    picks, both = call(
         functools.partial(list_kernel, cap, tiles),
-        jax.ShapeDtypeStruct((2, parts * tiles + 16), jnp.int32),
-        [smem, smem],
-        smem,
+        (jax.ShapeDtypeStruct((2, parts * tiles + 16), jnp.int32), both_array),
+        [smem, smem, vmem, vmem],
+        (smem, vmem),
         [pltpu.SMEM((parts,), jnp.int32)],
         1 << 24,
-    )(slots, block_region)
-
-    part, share_lo, share_hi = call(
-        functools.partial(contact_kernel, tiles),
-        (node_array, share, share),
-        [smem] + [vmem] * 6,
-        (vmem, vmem, vmem),
-        [],
-        1 << 28,
-    )(picks, back.reshape(-1, lanes), surf_nodes, part, mass, shared_lo, shared_hi)
+    )(slots, block_region, shared_lo, shared_hi)
+
+    part = call(
+        functools.partial(contact_kernel, tiles), node_array, [smem] + [vmem] * 3, vmem, [], 1 << 28
+    )(picks, back.reshape(-1, lanes), surf_nodes, part)
+    pair, share_lo, share_hi = call(
+        pair_kernel, (node_array, share, share), [vmem] * 4, (vmem, vmem, vmem), [], 1 << 28
+    )(part, from_mate(part, 1), mass, both)
     from_upper = shifted(share_lo, "dom", -1)
     from_lower = shifted(share_hi, "dom", 1)
 
     own, own_mass = call(
-        share_kernel, (node_array, mass_array), [vmem] * 6, (vmem, vmem), [], 1 << 28
-    )(part, mass, from_upper, from_lower, shared_lo, shared_hi)
-    others = [
-        lax.ppermute(own, "rep", [(i, i ^ k) for i in range(mates)]) for k in range(1, mates)
-    ]
-    accel = call(accel_kernel, node_array, [vmem] * (2 + len(others)), vmem, [], 1 << 24)(
-        own_mass, own, *others
+        share_kernel, (node_array, mass_array), [vmem] * 5, (vmem, vmem), [], 1 << 28
+    )(pair, mass, from_upper, from_lower, both)
+    distance = 2
+    while 2 * distance < mates:
+        own = own + from_mate(own, distance)
+        distance *= 2
+    accel = call(accel_kernel, node_array, [vmem] * 3, vmem, [], 1 << 24)(
+        own_mass, own, from_mate(own, distance)
     )
     return accel.reshape(1, 3, nodes_all)
 

time: 54.3 us -> 48.6 us (0.90)
  the two profiles are of different devices: /device:TPU:9 before, /device:TPU:0 now
where the time goes in v1:
time: 48.6 us; the launch traced here: 47.9 us
  starting transfers between devices  18.3 us (38%)
  waiting for transfers between devices  14.6 us (30%)
  Pallas kernels  14.2 us (29%)
  local copies, waits for them, and re-layouts  0.66 us (1%)
    all_to_all x1, starting transfers between devices, on_device(): lax.all_to_all(outgoing, 'dom', split_axis=0, concat_axis=0, tiled=True)  7.43 us
    ppermute x2, starting transfers between devices, shifted(): return lax.ppermute(block, axis, route)  5.84 us
    all_to_all x1, waiting for transfers between devices, on_device(): lax.all_to_all(forces, 'dom', split_axis=0, concat_axis=0, tiled=True)  5.17 us
    ppermute x2, waiting for transfers between devices, from_mate(): lax.ppermute(block, 'rep', [(i, i ^ distance) for i in range(lax.axis_siz...  4.41 us
    pallas_call x1, Pallas kernels, on_device(): call(functools.partial(pack_kernel, cap), jax.ShapeDtypeStruct((parts, ro...  4.33 us
    pallas_call x1, Pallas kernels, on_device(): call(functools.partial(element_kernel, cap, rows), (node_array, jax.Shape...  4.08 us
    all_to_all x1, waiting for transfers between devices, on_device(): lax.all_to_all(outgoing, 'dom', split_axis=0, concat_axis=0, tiled=True)  3.67 us
    all_to_all x1, starting transfers between devices, on_device(): lax.all_to_all(forces, 'dom', split_axis=0, concat_axis=0, tiled=True)  3.37 us
  transfers between devices with their start and end apart: 6, of which 5 were waited for; matrix products, arithmetic and copies ran while one was open for 0% of the time, Pallas kernels for 12%

profile of v1, /device:TPU:0, one launch (start us, length us, event | category | flops | bytes accessed | tf_op | source)
XLA Modules:
  0.0 47.9 jit_solution(185565083259923680)
XLA Ops:
  0.0 4.3 %shard_map.146 = bf16[8,112,128]{2,1,0:T(8,128)(2,1)} custom-call(s32[1,128]{1,0:T(1,128)} %region_ref.1, s32[1,8]{1,0:T(1,128)} %slot_hbm.1, f32[192,128]{1,0:T(8,128)} %bitcast.18, f32[192,128]{1,0:T(8,128)} %bitcast.12, s32[1,128,128]{2,1,0:T(8,128)} %surf_ref.1), custom_call_target="tpu_custom_call" | custom-call | flops 1073741824 | bytes 1048576 | tf_op jit(solution)/shard_map/pallas_call | solution.py:348
  4.3 0.0 copy-start.1
  4.4 0.0 copy-start.2
  4.4 0.0 copy-start.3
  4.4 0.0 copy-start.5
  4.4 0.0 copy-start.7
  4.4 0.0 copy-start.8
  4.4 7.4 %all-to-all-start = ((bf16[8,112,128]{2,1,0:T(8,128)(2,1)}), bf16[8,112,128]{2,1,0:T(8,128)(2,1)S(1)}, u32[]{:S(2)}, u32[]{:S(2)}) async-start(bf16[8,112,128]{2,1,0:T(8,128)(2,1)} %shard_map.146), calls=%async_computation | async-start | bytes 458752 | tf_op jit(solution)/shard_map/all_to_all | solution.py:365
  11.8 0.0 copy-start.12
  11.9 0.0 copy-done.1
  11.9 0.6 %copy-done.11 = s32[1,8]{1,0:T(1,128)S(1)} copy-done((s32[1,8]{1,0:T(1,128)S(1)}, s32[1,8]{1,0:T(1,128)}, u32[]{:S(2)}) %copy-start.11) | copy-done | bytes 56
  12.5 0.0 copy-done.12
  12.5 4.1 %shard_map.145 = (f32[192,128]{1,0:T(8,128)S(1)}, f32[2,24,128]{2,1,0:T(8,128)S(1)}, s32[1,8]{1,0:T(1,128)S(1)}) custom-call(s32[1,8]{1,0:T(1,128)S(1)} %copy-done.11, s32[1,8]{1,0:T(1,128)S(1)} %copy-done.12, f32[1,3,64,128]{3,2,1,0:T(8,128)S(1)} %bitcast.10, f32[1,3,64,128]{3,2,1,0:T(8,128)S(1)} %bitcast.11, f32[192,128]{1,0:T(8,128)S(1)} %bitcast.13, ...), custom_call_target="tpu_custom_call" | custom-call | flops 4294967296 | bytes 1048576 | tf_op jit(solution)/shard_map/pallas_call | solution.py:367
  16.6 3.7 %all-to-all-done.got_ref = bf16[8,112,128]{2,1,0:T(8,128)(2,1)S(1)} async-done(((bf16[8,112,128]{2,1,0:T(8,128)(2,1)}), bf16[8,112,128]{2,1,0:T(8,128)(2,1)S(1)}, u32[]{:S(2)}, u32[]{:S(2)}) %all-to-all-start) | async-done | bytes 229408 | tf_op jit(solution)/shard_map/all_to_all | solution.py:365
  20.3 1.6 %shard_map.147 = (f32[8,24,128]{2,1,0:T(8,128)}, s32[8,128]{1,0:T(8,128)S(1)}) custom-call(s32[1,8]{1,0:T(1,128)S(1)} %get-tuple-element.17.starts_ref, bf16[8,112,128]{2,1,0:T(8,128)(2,1)S(1)} %all-to-all-done.got_ref, f32[2,24,128]{2,1,0:T(8,128)S(1)} %get-tuple-element.18.faces_ref, bf16[1,8,128,128]{3,2,1,0:T(8,128)(2,1)S(1)} %copy-done), custom_call_target="tpu_custom_call" | custom-call | flops 268435456 | bytes 1048576 | tf_op jit(solution)/shard_map/pallas_call | solution.py:392
  21.9 3.4 %all-to-all-start.1 = ((f32[8,24,128]{2,1,0:T(8,128)}), f32[8,24,128]{2,1,0:T(8,128)S(1)}, u32[]{:S(2)}, u32[]{:S(2)}) async-start(f32[8,24,128]{2,1,0:T(8,128)} %get-tuple-element.21), calls=%async_computation.1 | async-start | bytes 196608 | tf_op jit(solution)/shard_map/all_to_all | solution.py:403
  25.2 0.0 copy-start.4
  25.3 1.9 %shard_map.148 = (s32[2,80]{1,0:T(2,128)S(1)}, s32[8,128]{1,0:T(8,128)S(1)}) custom-call(s32[8,128]{1,0:T(8,128)S(1)} %get-tuple-element.19.slots_ref, s32[1,128]{1,0:T(1,128)S(1)} %copy-done.13, s32[4,128]{1,0:T(4,128)S(1)} %bitcast.16, s32[4,128]{1,0:T(4,128)S(1)} %bitcast.17), custom_call_target="tpu_custom_call" | custom-call | flops 16777216 | bytes 1048576 | tf_op jit(solution)/shard_map/pallas_call | solution.py:405
  27.2 5.2 %all-to-all-done.1 = f32[8,24,128]{2,1,0:T(8,128)S(1)} async-done(((f32[8,24,128]{2,1,0:T(8,128)}), f32[8,24,128]{2,1,0:T(8,128)S(1)}, u32[]{:S(2)}, u32[]{:S(2)}) %all-to-all-start.1) | async-done | bytes 98336 | tf_op jit(solution)/shard_map/all_to_all | solution.py:403
  32.4 0.9 %shard_map.149.part_ref = f32[192,128]{1,0:T(8,128)S(1)} custom-call(s32[2,80]{1,0:T(2,128)S(1)} %get-tuple-element.20.list_ref, f32[192,128]{1,0:T(8,128)S(1)} %bitcast.9, s32[1,128,128]{2,1,0:T(8,128)S(1)} %copy-done.4, f32[192,128]{1,0:T(8,128)S(1)} %get-tuple-element.22.part_ref), custom_call_target="tpu_custom_call" | custom-call | flops 268435456 | bytes 1048576 | tf_op jit(solution)/shard_map/pallas_call | solution.py:414
  33.3 0.1 collective-permute-start
  33.4 1.3 %collective-permute-done.other_ref = f32[192,128]{1,0:T(8,128)S(1)} collective-permute-done((f32[192,128]{1,0:T(8,128)S(1)}, f32[192,128]{1,0:T(8,128)S(1)}, u32[]{:S(2)}, u32[]{:S(2)}) %collective-permute-start) | collective-permute-done | bytes 98336 | tf_op jit(solution)/shard_map/ppermute | solution.py:310
  34.7 0.0 copy-done.6
  34.7 0.3 shard_map.150
  35.0 1.3 %collective-permute-start.1 = (f32[16,128]{1,0:T(8,128)S(1)}, f32[16,128]{1,0:T(8,128)S(1)}, u32[]{:S(2)}, u32[]{:S(2)}) collective-permute-start(f32[16,128]{1,0:T(8,128)S(1)} %get-tuple-element.25), channel_id=1, source_target_pairs={{4,0},{8,4},{12,8},{16,12},{20,16},{24,20},{28,24},{5,1},{9,5},{13... | collective-permute-start | bytes 24584 | tf_op jit(solution)/shard_map/ppermute | solution.py:306
  36.3 4.5 %collective-permute-start.2 = (f32[16,128]{1,0:T(8,128)S(1)}, f32[16,128]{1,0:T(8,128)S(1)}, u32[]{:S(2)}, u32[]{:S(2)}) collective-permute-start(f32[16,128]{1,0:T(8,128)S(1)} %get-tuple-element.26), channel_id=1, source_target_pairs={{0,4},{4,8},{8,12},{12,16},{16,20},{20,24},{24,28},{1,5},{5,9},{9,... | collective-permute-start | bytes 24584 | tf_op jit(solution)/shard_map/ppermute | solution.py:306
  40.8 0.0 collective-permute-done.1.up_ref
  40.9 1.3 %collective-permute-done.2.down_ref = f32[16,128]{1,0:T(8,128)S(1)} collective-permute-done((f32[16,128]{1,0:T(8,128)S(1)}, f32[16,128]{1,0:T(8,128)S(1)}, u32[]{:S(2)}, u32[]{:S(2)}) %collective-permute-start.2) | collective-permute-done | bytes 8224 | tf_op jit(solution)/shard_map/ppermute | solution.py:306
  42.2 0.4 shard_map.151
  42.6 1.6 %collective-permute-start.3 = (f32[192,128]{1,0:T(8,128)S(1)}, f32[192,128]{1,0:T(8,128)S(1)}, u32[]{:S(2)}, u32[]{:S(2)}) collective-permute-start(f32[192,128]{1,0:T(8,128)S(1)} %get-tuple-element.28.own_ref), channel_id=1, source_target_pairs={{0,2},{1,3},{2,0},{3,1},{4,6},{5,7},{6,4},{7,5},{8,10},{9,11},{10,... | collective-permute-start | bytes 294920 | tf_op jit(solution)/shard_map/ppermute | solution.py:310
  44.1 3.1 %collective-permute-done.3.other_ref = f32[192,128]{1,0:T(8,128)S(1)} collective-permute-done((f32[192,128]{1,0:T(8,128)S(1)}, f32[192,128]{1,0:T(8,128)S(1)}, u32[]{:S(2)}, u32[]{:S(2)}) %collective-permute-start.3) | collective-permute-done | bytes 98336 | tf_op jit(solution)/shard_map/ppermute | solution.py:310
  47.3 0.7 %shard_map.152 = f32[192,128]{1,0:T(8,128)} custom-call(f32[64,128]{1,0:T(8,128)S(1)} %get-tuple-element.27.mass_ref, f32[192,128]{1,0:T(8,128)S(1)} %get-tuple-element.28.own_ref, f32[192,128]{1,0:T(8,128)S(1)} %collective-permute-done.3.other_ref), custom_call_target="tpu_custom_call" | custom-call | flops 16777216 | bytes 1048576 | tf_op jit(solution)/shard_map/pallas_call | solution.py:430
  (16 shorter events, 0.0 us)
Async XLA Ops:
  4.3 7.5 %copy-start.1 = (f32[1,64,3,128]{3,1,2,0:T(8,128)S(1)}, f32[1,64,3,128]{3,1,2,0:T(8,128)}, u32[]{:S(2)}) copy-start(f32[1,64,3,128]{3,1,2,0:T(8,128)} %param.23) | copy-start | bytes 294916
  4.4 7.5 %copy-start.2 = (f32[1,64,3,128]{3,1,2,0:T(8,128)S(1)}, f32[1,64,3,128]{3,1,2,0:T(8,128)}, u32[]{:S(2)}) copy-start(f32[1,64,3,128]{3,1,2,0:T(8,128)} %param.24) | copy-start | bytes 294916
  4.4 7.5 %copy-start.3 = (f32[1,3,8192]{2,0,1:T(1,128)S(1)}, f32[1,3,8192]{2,0,1:T(1,128)}, u32[]{:S(2)}) copy-start(f32[1,3,8192]{2,0,1:T(1,128)} %param.16) | copy-start | bytes 294916
  4.4 7.5 %copy-start.5 = (s32[1,8,1024]{2,1,0:T(8,128)S(1)}, s32[1,8,1024]{2,1,0:T(8,128)}, u32[]{:S(2)}) copy-start(s32[1,8,1024]{2,1,0:T(8,128)} %nodes_ref.1) | copy-start | bytes 98308
  4.4 7.5 %copy-start.7 = (f32[24,24]{1,0:T(8,128)S(1)}, f32[24,24]{1,0:T(8,128)}, u32[]{:S(2)}) copy-start(f32[24,24]{1,0:T(8,128)} %stiff_ref.1) | copy-start | bytes 6916
  4.4 7.5 %copy-start.8 = (f32[1,1024]{1,0:T(1,128)S(1)}, f32[1,1024]{1,0:T(1,128)}, u32[]{:S(2)}) copy-start(f32[1,1024]{1,0:T(1,128)} %modulus_ref.1) | copy-start | bytes 12292
  4.4 15.9 %all-to-all-start = ((bf16[8,112,128]{2,1,0:T(8,128)(2,1)}), bf16[8,112,128]{2,1,0:T(8,128)(2,1)S(1)}, u32[]{:S(2)}, u32[]{:S(2)}) async-start(bf16[8,112,128]{2,1,0:T(8,128)(2,1)} %shard_map.146), calls=%async_computation | async-start | bytes 458752 | tf_op jit(solution)/shard_map/all_to_all | solution.py:365
  11.8 0.7 %copy-start.11 = (s32[1,8]{1,0:T(1,128)S(1)}, s32[1,8]{1,0:T(1,128)}, u32[]{:S(2)}) copy-start(s32[1,8]{1,0:T(1,128)} %slot_hbm.1) | copy-start | bytes 100
  11.8 0.7 %copy-start.12 = (s32[1,8]{1,0:T(1,128)S(1)}, s32[1,8]{1,0:T(1,128)}, u32[]{:S(2)}) copy-start(s32[1,8]{1,0:T(1,128)} %face_ref.1) | copy-start | bytes 100
  12.5 7.8 %copy-start = (bf16[1,8,128,128]{3,2,1,0:T(8,128)(2,1)S(1)}, bf16[1,8,128,128]{3,2,1,0:T(8,128)(2,1)}, u32[]{:S(2)}) copy-start(bf16[1,8,128,128]{3,2,1,0:T(8,128)(2,1)} %weight_ref.1) | copy-start | bytes 786436
  20.3 5.0 %copy-start.9 = (s32[1,512]{1,0:T(1,128)S(1)}, s32[1,512]{1,0:T(1,128)}, u32[]{:S(2)}) copy-start(s32[1,512]{1,0:T(1,128)} %param.28) | copy-start | bytes 6148
  20.3 5.0 %copy-start.10 = (s32[1,512]{1,0:T(1,128)S(1)}, s32[1,512]{1,0:T(1,128)}, u32[]{:S(2)}) copy-start(s32[1,512]{1,0:T(1,128)} %param.29) | copy-start | bytes 6148
  20.3 5.0 %copy-start.13 = (s32[1,128]{1,0:T(1,128)S(1)}, s32[1,128]{1,0:T(1,128)}, u32[]{:S(2)}) copy-start(s32[1,128]{1,0:T(1,128)} %region_ref.1) | copy-start | bytes 1540
  21.9 10.5 %all-to-all-start.1 = ((f32[8,24,128]{2,1,0:T(8,128)}), f32[8,24,128]{2,1,0:T(8,128)S(1)}, u32[]{:S(2)}, u32[]{:S(2)}) async-start(f32[8,24,128]{2,1,0:T(8,128)} %get-tuple-element.21), calls=%async_computation.1 | async-start | bytes 196608 | tf_op jit(solution)/shard_map/all_to_all | solution.py:403
  25.2 7.1 %copy-start.4 = (s32[1,128,128]{2,1,0:T(8,128)S(1)}, s32[1,128,128]{2,1,0:T(8,128)}, u32[]{:S(2)}) copy-start(s32[1,128,128]{2,1,0:T(8,128)} %surf_ref.1) | copy-start | bytes 196612
  32.3 2.3 %copy-start.6 = (f32[1,8192]{1,0:T(1,128)S(1)}, f32[1,8192]{1,0:T(1,128)}, u32[]{:S(2)}) copy-start(f32[1,8192]{1,0:T(1,128)} %param.17) | copy-start | bytes 98308
  33.3 1.4 %collective-permute-start = (f32[192,128]{1,0:T(8,128)S(1)}, f32[192,128]{1,0:T(8,128)S(1)}, u32[]{:S(2)}, u32[]{:S(2)}) collective-permute-start(f32[192,128]{1,0:T(8,128)S(1)} %shard_map.149.part_ref), channel_id=1, source_target_pairs={{0,1},{1,0},{2,3},{3,2},{4,5},{5,4},{6,7},{7,6},{8,9},{9,8},{10,11... | collective-permute-start | bytes 294920 | tf_op jit(solution)/shard_map/ppermute | solution.py:310
  35.0 5.9 %collective-permute-start.1 = (f32[16,128]{1,0:T(8,128)S(1)}, f32[16,128]{1,0:T(8,128)S(1)}, u32[]{:S(2)}, u32[]{:S(2)}) collective-permute-start(f32[16,128]{1,0:T(8,128)S(1)} %get-tuple-element.25), channel_id=1, source_target_pairs={{4,0},{8,4},{12,8},{16,12},{20,16},{24,20},{28,24},{5,1},{9,5},{13... | collective-permute-start | bytes 24584 | tf_op jit(solution)/shard_map/ppermute | solution.py:306
  36.3 5.9 %collective-permute-start.2 = (f32[16,128]{1,0:T(8,128)S(1)}, f32[16,128]{1,0:T(8,128)S(1)}, u32[]{:S(2)}, u32[]{:S(2)}) collective-permute-start(f32[16,128]{1,0:T(8,128)S(1)} %get-tuple-element.26), channel_id=1, source_target_pairs={{0,4},{4,8},{8,12},{12,16},{16,20},{20,24},{24,28},{1,5},{5,9},{9,... | collective-permute-start | bytes 24584 | tf_op jit(solution)/shard_map/ppermute | solution.py:306
  42.6 4.7 %collective-permute-start.3 = (f32[192,128]{1,0:T(8,128)S(1)}, f32[192,128]{1,0:T(8,128)S(1)}, u32[]{:S(2)}, u32[]{:S(2)}) collective-permute-start(f32[192,128]{1,0:T(8,128)S(1)} %get-tuple-element.28.own_ref), channel_id=1, source_target_pairs={{0,2},{1,3},{2,0},{3,1},{4,6},{5,7},{6,4},{7,5},{8,10},{9,11},{10,... | collective-permute-start | bytes 294920 | tf_op jit(solution)/shard_map/ppermute | solution.py:310
